TPU v7x, 32 devices: a whole 2x2x4 slice. The times are simulated.
32 devices in a mesh: groups: 2 (over y), rows: 8 (over z, x), cols: 2 (over core).
Axes of the slice: x: 2, y: 2, z: 4, core: 2. Of those that a mesh axis runs over, the one named last changes fastest.
Arguments:
- query_grad: float32 [65536, 4096], P(('groups', 'rows'), 'cols'), parts along dimension 0, may hold values from -6 to 6
- out_basis: float32 [32768, 256], P('rows'), may hold values from -0.03125 to 0.03125
- in_basis: float32 [4096, 4096], P('cols', 'rows'), may hold values from -0.09375 to 0.09375
- eigenvalues: float32 [256, 4096], P(None, 'rows'), may hold values from 0.01 to 64, as said below
Outputs:
- inverse_product: float32 [65536, 4096], P(('groups', 'rows'), 'cols'), parts along dimension 0
There are 2 independent parts, one for each index of `groups`. A program takes and returns all parts, laid end to end along the dimension named above; an argument that names none is the same for every part. Nothing has to cross between parts.
Inputs may be any that keep to these rules, and one draw needn't show every extreme that they name: `eigenvalues`: positive.
All inputs are finite; a program needn't handle non-finite values.
Results may differ from a plain program's by a relative error of at most 0.000062.
Values sent between devices are 32-bit elements; how exact they have to be, the bound alone decides.
A program may use at most 256 MiB of HBM per device.

v0:
```python
import jax
import jax.numpy as jnp
from jax import lax
from jax.sharding import PartitionSpec as P

PIN = 4096
WIN = 256


precise = lax.Precision.HIGHEST


def per_device(query_grad, out_basis, in_basis, eigenvalues):
    local_total = jnp.sum(eigenvalues)
    reduced = lax.psum_scatter(
        lax.dot_general(
            out_basis,
            query_grad,
            (((0,), (0,)), ((), ())),
            precision=precise,
            preferred_element_type=jnp.float32,
        ),
        "rows",
        scatter_dimension=0,
        tiled=True,
    )
    projected = lax.all_gather(reduced, "rows", axis=0, tiled=True)
    overall = lax.psum(local_total, "rows")
    damping = 0.1 * (overall / (WIN * PIN))
    rotated = jnp.dot(projected, in_basis, precision=precise, preferred_element_type=jnp.float32)
    summed = lax.psum(rotated, "cols")
    scaled = summed / (eigenvalues + damping)
    returned = lax.dot_general(
        scaled,
        in_basis,
        (((1,), (1,)), ((), ())),
        precision=precise,
        preferred_element_type=jnp.float32,
    )
    returned = lax.psum(returned, "rows")
    return jnp.dot(out_basis, returned, precision=precise, preferred_element_type=jnp.float32)


def solution(mesh):
    return jax.shard_map(
        per_device,
        mesh=mesh,
        in_specs=(
            P(("groups", "rows"), "cols"),
            P("rows", None),
            P("cols", "rows"),
            P(None, "rows"),
        ),
        out_specs=P(("groups", "rows"), "cols"),
        check_vma=False,
    )
```

profile of v0, /device:TPU:0, one launch (start us, length us, event | category | flops | bytes accessed | tf_op | source)
XLA Modules:
  0.0 394.9 jit_solution(9805601765475856413)
XLA Ops:
  6.5 0.0 reduce-scatter.2.cloned.1.call-start
  6.5 33.8 %fusion.4 = f32[256,2048]{1,0:T(8,128)} fusion(f32[4096,256]{1,0:T(8,128)} %param.5, f32[4096,2048]{1,0:T(8,128)} %param.4), kind=kOutput, calls=%fused_computation.5 | convolution fusion | flops 25769803776 | bytes 39845888 | tf_op jit(solution)/shard_map/dot_general | solution.py:16
  40.3 0.0 reduce-scatter.2.cloned.1.call-update
  40.4 0.0 copy-start
  40.4 0.0 all-gather.2.cloned.1.call-start
  40.4 70.9 %reduce-scatter.2.cloned.1.call-done = f32[32,2048]{1,0:T(8,128)} async-done(((f32[256,2048]{1,0:T(8,128)}), f32[32,2048]{1,0:T(8,128)}) %reduce-scatter.2.cloned.1.call-update) | async-done | bytes 262160 | tf_op jit(solution)/shard_map/reduce_scatter | solution.py:15
  111.3 0.0 all-gather.2.cloned.1.call-update
  111.3 0.0 all-reduce.3.cloned.1.call-start
  111.4 50.4 %all-gather.2.cloned.1.call-done = f32[256,2048]{1,0:T(8,128)} async-done(((f32[32,2048]{1,0:T(8,128)}), f32[256,2048]{1,0:T(8,128)}) %all-gather.2.cloned.1.call-update) | async-done | bytes 2097168 | tf_op jit(solution)/shard_map/all_gather | solution.py:27
  161.8 7.3 %fusion.5 = f32[256,512]{1,0:T(8,128)} fusion(f32[256,2048]{1,0:T(8,128)} %all-gather.2.cloned.1.call-done, f32[2048,512]{1,0:T(8,128)} %param.6), kind=kOutput, calls=%fused_computation.6 | convolution fusion | flops 3221225472 | bytes 6815744 | tf_op jit(solution)/shard_map/dot_general | solution.py:30
  169.1 0.0 all-reduce.3.cloned.1.call-update
  169.1 0.0 all-reduce.5.cloned.1.call-start
  169.1 0.0 copy-done
  169.2 0.8 reduce_sum.9
  170.0 19.8 %psum.22 = f32[]{:T(128)} all-reduce(f32[]{:T(128)} %reduce_sum.9), channel_id=1, replica_groups=mesh['groups'=2,'rows'=8,'cols'=2] {'rows'}, use_global_device_ids=true, to_apply=%region_3.0 | all-reduce | flops 1 | bytes 8 | tf_op jit(solution)/shard_map/psum | solution.py:28
  190.5 0.0 all-reduce.3.cloned.1.call-done
  190.5 7.3 %fusion = f32[256,2048]{1,0:T(8,128)} fusion(f32[2048,512]{1,0:T(8,128)} %param.6, f32[256,512]{1,0:T(8,128)} %all-reduce.3.cloned.1.call-done, f32[256,512]{1,0:T(8,128)S(1)} %copy-done, f32[]{:T(128)S(6)} %mul_shard_map.3), kind=kOutput, calls=%fused_computation.1 | convolution fusion | flops 3221487616 | bytes 7340036 | tf_op jit(solution)/shard_map/dot_general | solution.py:33
  197.8 0.0 all-reduce.5.cloned.1.call-update
  197.8 99.2 %all-reduce.5.cloned.1.call-done = f32[256,2048]{1,0:T(8,128)} async-done(((f32[256,2048]{1,0:T(8,128)}), f32[256,2048]{1,0:T(8,128)}) %all-reduce.5.cloned.1.call-update) | async-done | bytes 2097168 | tf_op jit(solution)/shard_map/psum | solution.py:40
  297.1 58.0 %convolution_bitcast_fusion = f32[4096,2048]{0,1:T(8,128)} fusion(f32[256,2048]{1,0:T(8,128)} %all-reduce.5.cloned.1.call-done, f32[4096,256]{1,0:T(8,128)} %param.5), kind=kOutput, calls=%fused_computation | convolution fusion | flops 25769803776 | bytes 39845888 | tf_op jit(solution)/shard_map/dot_general | solution.py:41
  355.1 33.3 %copy.5 = f32[4096,2048]{1,0:T(8,128)} copy(f32[4096,2048]{0,1:T(8,128)} %convolution_bitcast_fusion) | data formatting | bytes 67108864 | tf_op jit(solution)/shard_map/dot_general | solution.py:41
Async XLA Ops:
  6.5 104.8 %reduce-scatter.2.cloned.1.call-start = ((), (), s32[]{:S(2)}) async-start(), calls=%async_computation.1 | async-start | bytes 2359296 | tf_op jit(solution)/shard_map/reduce_scatter | solution.py:15
  40.4 128.8 %copy-start = (f32[256,512]{1,0:T(8,128)S(1)}, f32[256,512]{1,0:T(8,128)}, u32[]{:S(2)}) copy-start(f32[256,512]{1,0:T(8,128)} %param.7) | copy-start | bytes 1572868
  40.4 121.4 %all-gather.2.cloned.1.call-start = ((), (), s32[]{:S(2)}) async-start(), calls=%async_computation.2 | async-start | bytes 2359296 | tf_op jit(solution)/shard_map/all_gather | solution.py:27
  111.3 79.1 %all-reduce.3.cloned.1.call-start = ((), (), s32[]{:S(2)}) async-start(), calls=%async_computation.3 | async-start | bytes 1048576 | tf_op jit(solution)/shard_map/psum | solution.py:31
  169.1 128.0 %all-reduce.5.cloned.1.call-start = ((), (), s32[]{:S(2)}) async-start(), calls=%async_computation.4 | async-start | bytes 4194304 | tf_op jit(solution)/shard_map/psum | solution.py:40
Sparse Core Ops, SparseCore 0:
  40.5 70.7 reduce-scatter.1
  113.4 48.2 all-gather.1
  169.2 17.2 all-reduce.2
  198.0 99.0 all-reduce.4
where the time goes:
time: 396 us; the launch traced here: 395 us
  waiting for transfers between devices  221 us (56%)
  matrix products  106 us (27%)
  local copies, waits for them, and re-layouts  33.3 us (8%)
  blocking collectives  19.8 us (5%)
  between operations  13.8 us (3%)
    psum x1, waiting for transfers between devices, per_device(): returned = lax.psum(returned, 'rows')  99.2 us
    reduce_scatter x1, waiting for transfers between devices, per_device(): lax.psum_scatter(lax.dot_general(out_basis, query_grad, (((0,), (0,)), ((...  70.9 us
    dot_general x1, matrix products, per_device(): jnp.dot(out_basis, returned, precision=precise, preferred_element_type=jn...  58 us
    all_gather x1, waiting for transfers between devices, per_device(): projected = lax.all_gather(reduced, 'rows', axis=0, tiled=True)  50.4 us
    dot_general x1, matrix products, per_device(): lax.dot_general(out_basis, query_grad, (((0,), (0,)), ((), ())), precisio...  33.8 us
    dot_general x1, local copies, waits for them, and re-layouts, per_device(): jnp.dot(out_basis, returned, precision=precise, preferred_element_type=jn...  33.3 us
    psum x1, blocking collectives, per_device(): overall = lax.psum(local_total, 'rows')  19.8 us
  transfers between devices with their start and end apart: 4, of which 3 were waited for; matrix products, arithmetic and copies ran while one was open for 0% of the time, Pallas kernels for 0%

commit v1 on v0

v1 whole, which is shorter than its diff:
```python
import functools

import jax
import jax.numpy as jnp
from jax import lax
from jax.experimental import pallas as pl
from jax.experimental.pallas import tpu as pltpu
from jax.sharding import PartitionSpec as P

precise = lax.Precision.HIGHEST
MESH = pl.DeviceIdType.MESH
RING = 8
LANES = 128
MIB = 1024 * 1024


def split(x):
    high = x.astype(jnp.bfloat16)
    low = (x - high.astype(jnp.float32)).astype(jnp.bfloat16)
    return high, low


def dot(a, b, contract=((1,), (0,))):
    return lax.dot_general(a, b, (contract, ((), ())), preferred_element_type=jnp.float32)


def ring_kernel(
    count,
    grad,
    out_basis,
    in_basis,
    eigen,
    result,
    grad_buf,
    basis_t_high,
    basis_t_low,
    basis_in,
    eig,
    ring_a,
    ring_b,
    rotated,
    rotated_peer,
    scaled_high,
    scaled_low,
    totals,
    basis_out,
    grad_sem,
    local_sem,
    send_a,
    recv_a,
    send_b,
    recv_b,
    send_t,
    recv_t,
    send_c,
    recv_c,
):
    row = lax.axis_index("rows")
    col = lax.axis_index("cols")
    depth = grad.shape[0]
    slots = grad_buf.shape[0]

    z, x = row // 2, row % 2
    place = z + x * (RING - 1 - 2 * z)

    def row_of(position):
        return 2 * position + (position // 4) * (2 * RING - 1 - 4 * position)

    right = row_of((place + 1) % RING)
    left = row_of((place + RING - 1) % RING)

    def chunk(direction, step):
        turn = (place + 2 * RING - step) if direction == 0 else (place + step)
        return pl.multiple_of((turn % RING) * (2 * LANES) + direction * LANES, LANES)

    def fetch(step, direction):
        return pltpu.make_async_copy(
            grad.at[:, pl.ds(chunk(direction, step), LANES)],
            grad_buf.at[step % slots, direction],
            grad_sem.at[step % slots, direction],
        )

    load_basis = pltpu.make_async_copy(out_basis, basis_out, local_sem.at[0])
    load_eig = pltpu.make_async_copy(eigen, eig, local_sem.at[1])
    load_in = pltpu.make_async_copy(in_basis, basis_in, local_sem.at[2])
    load_basis.start()
    for step in range(slots):
        for direction in range(2):
            fetch(step, direction).start()
        if step == 0:
            load_eig.start()
            load_in.start()

    barrier = pltpu.get_barrier_semaphore()
    for offset in range(1, RING):
        pl.semaphore_signal(
            barrier, inc=1, device_id={"rows": (row + offset) % RING}, device_id_type=MESH
        )
    pl.semaphore_signal(barrier, inc=1, device_id={"cols": 1 - col}, device_id_type=MESH)

    load_basis.wait()
    piece = min(512, depth)
    for start in range(0, depth, piece):
        high, low = split(basis_out[start : start + piece, :].T)
        basis_t_high[:, start : start + piece] = high
        basis_t_low[:, start : start + piece] = low

    load_eig.wait()
    sums = jnp.sum(eig[...], axis=0, keepdims=True)
    lane_sums = sums[:, 0:LANES]
    for start in range(LANES, eig.shape[1], LANES):
        lane_sums = lane_sums + sums[:, start : start + LANES]
    totals[pl.ds(row, 1)] = jnp.broadcast_to(lane_sums, (8, LANES))[None]

    pl.semaphore_wait(barrier, RING)

    def total_copy(offset):
        return pltpu.make_async_remote_copy(
            src_ref=totals.at[row],
            dst_ref=totals.at[row],
            send_sem=send_t.at[offset - 1],
            recv_sem=recv_t.at[offset - 1],
            device_id={"rows": (row + offset) % RING},
            device_id_type=MESH,
        )

    for offset in range(1, RING):
        total_copy(offset).start()

    def hop(ring, send, recv, direction, step):
        return pltpu.make_async_remote_copy(
            src_ref=ring.at[direction, step],
            dst_ref=ring.at[direction, step + 1],
            send_sem=send.at[direction, step],
            recv_sem=recv.at[direction, step],
            device_id={"rows": right if direction == 0 else left},
            device_id_type=MESH,
        )

    def reduce_step(ring, send, recv, step, local):
        @pl.when(step == 0)
        def _():
            for direction in range(2):
                ring[direction, 0] = local[direction]
                hop(ring, send, recv, direction, 0).start()

        @pl.when(step > 0)
        def _():
            for direction in range(2):
                hop(ring, send, recv, direction, step - 1).wait_recv()
                ring[direction, step] = ring[direction, step] + local[direction]
                hop(ring, send, recv, direction, step).start()

    def project(step, carry):
        fetch(step, 0).wait()
        fetch(step, 1).wait()
        slot = step % slots
        local = [None, None]
        block = min(1024, depth)
        for start in range(0, depth, block):
            rows = slice(start, start + block)
            one_high, one_low = split(grad_buf[slot, 0, rows, :])
            two_high, two_low = split(grad_buf[slot, 1, rows, :])
            upper = jnp.concatenate([one_high, one_low, two_high, two_low], axis=1)
            wide = dot(basis_t_high[:, rows], upper)
            highs = jnp.concatenate([one_high, two_high], axis=1)
            narrow = dot(basis_t_low[:, rows], highs)
            for direction in range(2):
                at = 2 * direction * LANES
                term = (
                    wide[:, at : at + LANES]
                    + wide[:, at + LANES : at + 2 * LANES]
                    + narrow[:, direction * LANES : (direction + 1) * LANES]
                )
                local[direction] = term if start == 0 else local[direction] + term

        @pl.when(step + slots < RING)
        def _():
            fetch(step + slots, 0).start()
            fetch(step + slots, 1).start()

        reduce_step(ring_a, send_a, recv_a, step, local)
        return carry

    lax.fori_loop(0, RING, project, 0)

    load_in.wait()
    rotated[...] = jnp.zeros_like(rotated)

    def basis_rows(step):
        return jnp.concatenate(
            [basis_in[pl.ds(chunk(direction, step), LANES), :] for direction in range(2)], axis=0
        )

    def arrive(ring, send, recv, step):
        @pl.when(step >= RING)
        def _():
            for direction in range(2):
                hop(ring, send, recv, direction, step - 1).wait_recv()

                @pl.when(step < 2 * RING - 2)
                def _():
                    hop(ring, send, recv, direction, step).start()

    def rotate(step, carry):
        b_high, b_low = split(basis_rows(step))
        arrive(ring_a, send_a, recv_a, step)
        p_high, p_low = split(jnp.concatenate([ring_a[0, step], ring_a[1, step]], axis=1))
        rotated[...] += dot(
            jnp.concatenate([p_high, p_high, p_low], axis=1),
            jnp.concatenate([b_high, b_low, b_high], axis=0),
        )
        return carry

    lax.fori_loop(RING - 1, 2 * RING - 1, rotate, 0)

    swap = pltpu.make_async_remote_copy(
        src_ref=rotated,
        dst_ref=rotated_peer,
        send_sem=send_c,
        recv_sem=recv_c,
        device_id={"cols": 1 - col},
        device_id_type=MESH,
    )
    swap.start()
    for offset in range(1, RING):
        total_copy(offset).wait()
    overall = jnp.sum(totals[...], axis=0)[0:1, :]
    overall = jnp.sum(overall, axis=1, keepdims=True)
    divisor = eig[...] + 0.1 * (overall / count)
    swap.wait()
    high, low = split((rotated[...] + rotated_peer[...]) / divisor)
    scaled_high[...] = high
    scaled_low[...] = low

    def give_back(step, carry):
        b_high, b_low = split(basis_rows(step))
        s_high, s_low = scaled_high[...], scaled_low[...]
        both = ((1,), (1,))
        part = dot(s_high, b_high, both) + dot(s_high, b_low, both) + dot(s_low, b_high, both)
        reduce_step(ring_b, send_b, recv_b, step, [part[:, :LANES], part[:, LANES:]])
        return carry

    lax.fori_loop(0, RING, give_back, 0)

    def collect(step, carry):
        arrive(ring_b, send_b, recv_b, step)
        for direction in range(2):
            result[:, pl.ds(chunk(direction, step), LANES)] = ring_b[direction, step]
        return carry

    lax.fori_loop(RING - 1, 2 * RING - 1, collect, 0)

    def drain(step, carry):
        for direction in range(2):
            hop(ring_a, send_a, recv_a, direction, step).wait_send()
            hop(ring_b, send_b, recv_b, direction, step).wait_send()
        return carry

    lax.fori_loop(0, 2 * RING - 2, drain, 0)


def back_rotated(query_grad, out_basis, in_basis, eigenvalues, count):
    depth, columns = query_grad.shape
    window = out_basis.shape[1]
    directions = in_basis.shape[1]
    slots = 4
    hops = 2 * RING - 2
    dma = pltpu.SemaphoreType.DMA
    f32, bf16 = jnp.float32, jnp.bfloat16
    flops = 6 * window * columns * (depth + 2 * directions)
    return pl.pallas_call(
        functools.partial(ring_kernel, count),
        out_shape=jax.ShapeDtypeStruct((window, columns), f32),
        in_specs=[pl.BlockSpec(memory_space=pl.ANY)] * 4,
        out_specs=pl.BlockSpec(memory_space=pltpu.VMEM),
        scratch_shapes=[
            pltpu.VMEM((slots, 2, depth, LANES), f32),
            pltpu.VMEM((window, depth), bf16),
            pltpu.VMEM((window, depth), bf16),
            pltpu.VMEM((columns, directions), f32),
            pltpu.VMEM((window, directions), f32),
            pltpu.VMEM((2, hops + 1, window, LANES), f32),
            pltpu.VMEM((2, hops + 1, window, LANES), f32),
            pltpu.VMEM((window, directions), f32),
            pltpu.VMEM((window, directions), f32),
            pltpu.VMEM((window, directions), bf16),
            pltpu.VMEM((window, directions), bf16),
            pltpu.VMEM((RING, 8, LANES), f32),
            pltpu.VMEM((depth, window), f32),
            dma((slots, 2)),
            dma((3,)),
            dma((2, hops)),
            dma((2, hops)),
            dma((2, hops)),
            dma((2, hops)),
            dma((RING - 1,)),
            dma((RING - 1,)),
            dma,
            dma,
        ],
        compiler_params=pltpu.CompilerParams(
            collective_id=0, has_side_effects=True, vmem_limit_bytes=56 * MIB
        ),
        cost_estimate=pl.CostEstimate(
            flops=flops, bytes_accessed=4 * depth * (columns + window), transcendentals=0
        ),
        name="ring_kernel",
    )(query_grad, out_basis, in_basis, eigenvalues)


def expand_kernel(basis, returned, out, stacked):
    @pl.when(pl.program_id(0) == 0)
    def _():
        r_high, r_low = split(returned[...])
        stacked[...] = jnp.concatenate([r_high, r_low, r_high], axis=0)

    u_high, u_low = split(basis[...])
    out[...] = dot(jnp.concatenate([u_high, u_high, u_low], axis=1), stacked[...])


def expand(out_basis, returned):
    depth, window = out_basis.shape
    columns = returned.shape[1]
    tile = min(512, depth)
    return pl.pallas_call(
        expand_kernel,
        grid=(depth // tile,),
        out_shape=jax.ShapeDtypeStruct((depth, columns), jnp.float32),
        in_specs=[
            pl.BlockSpec((tile, window), lambda i: (i, 0)),
            pl.BlockSpec((window, columns), lambda i: (0, 0)),
        ],
        out_specs=pl.BlockSpec((tile, columns), lambda i: (i, 0)),
        scratch_shapes=[pltpu.VMEM((3 * window, columns), jnp.bfloat16)],
        compiler_params=pltpu.CompilerParams(vmem_limit_bytes=40 * MIB),
        cost_estimate=pl.CostEstimate(
            flops=6 * depth * window * columns,
            bytes_accessed=4 * depth * (columns + window),
            transcendentals=0,
        ),
        name="expand_kernel",
    )(out_basis, returned)


def with_collectives(query_grad, out_basis, in_basis, eigenvalues, count):
    def product(a, b, contract):
        return lax.dot_general(
            a, b, (contract, ((), ())), precision=precise, preferred_element_type=jnp.float32
        )

    projected = lax.psum(product(out_basis, query_grad, ((0,), (0,))), "rows")
    damping = 0.1 * (lax.psum(jnp.sum(eigenvalues), "rows") / count)
    rotated = lax.psum(product(projected, in_basis, ((1,), (0,))), "cols")
    scaled = rotated / (eigenvalues + damping)
    return lax.psum(product(scaled, in_basis, ((1,), (1,))), "rows")


def per_device(sizes, query_grad, out_basis, in_basis, eigenvalues):
    rows, cols = sizes
    count = eigenvalues.shape[0] * eigenvalues.shape[1] * rows
    on_ring = (
        rows == RING
        and cols == 2
        and query_grad.shape[1] == 2 * RING * LANES
        and eigenvalues.shape[1] % LANES == 0
    )
    inner = back_rotated if on_ring else with_collectives
    returned = inner(query_grad, out_basis, in_basis, eigenvalues, count)
    return expand(out_basis, returned)


def solution(mesh):
    return jax.shard_map(
        functools.partial(per_device, (mesh.shape["rows"], mesh.shape["cols"])),
        mesh=mesh,
        in_specs=(
            P(("groups", "rows"), "cols"),
            P("rows", None),
            P("cols", "rows"),
            P(None, "rows"),
        ),
        out_specs=P(("groups", "rows"), "cols"),
        check_vma=False,
    )
```

time: 396 us -> 165 us (0.42)
  waiting for transfers between devices: 221 us -> 0 us
  Pallas kernels: 0 us -> 163 us
  matrix products: 106 us -> 0 us
  local copies, waits for them, and re-layouts: 33.3 us -> 1.59 us
  blocking collectives: 19.8 us -> 0 us
  between operations: 13.8 us -> 0.03 us
    pallas_call x0 -> x2, Pallas kernels: none -> 163 us  [the longest x1 146 us: back_rotated(): pl.pallas_call(functools.partial(ring_kernel, count), out_shape=jax.Shape...]
    dot_general x4 -> x0, matrix products: 106 us -> none  [the longest x1 58 us: per_device(): jnp.dot(out_basis, returned, precision=precise, preferred_element_type=jn...]
    psum x2 -> x0, waiting for transfers between devices: 99.3 us -> none  [the longest x1 99.2 us: per_device(): returned = lax.psum(returned, 'rows')]
    reduce_scatter x1 -> x0, waiting for transfers between devices: 70.9 us -> none  [per_device(): lax.psum_scatter(lax.dot_general(out_basis, query_grad, (((0,), (0,)), ((...]
    all_gather x1 -> x0, waiting for transfers between devices: 50.4 us -> none  [per_device(): projected = lax.all_gather(reduced, 'rows', axis=0, tiled=True)]
    dot_general x1 -> x0, local copies, waits for them, and re-layouts: 33.3 us -> none  [per_device(): jnp.dot(out_basis, returned, precision=precise, preferred_element_type=jn...]
    psum x1 -> x0, blocking collectives: 19.8 us -> none  [per_device(): overall = lax.psum(local_total, 'rows')]
  transfers between devices with their start and end apart: 4 -> 0, of which waited for: 3 -> 0; matrix products, arithmetic and copies ran while one was open for 0% -> 0% of each run, Pallas kernels for 0% -> 0%
where the time goes in v1:
time: 165 us
  Pallas kernels  163 us (99%)
    pallas_call x1, Pallas kernels, back_rotated(): pl.pallas_call(functools.partial(ring_kernel, count), out_shape=jax.Shape...  146 us
    pallas_call x1, Pallas kernels, expand(): pl.pallas_call(expand_kernel, grid=(depth // tile,), out_shape=jax.ShapeD...  17.4 us

profile of v1, /device:TPU:0, one launch (start us, length us, event | category | flops | bytes accessed | tf_op | source)
XLA Modules:
  0.0 164.9 jit_solution(12722520666320184896)
XLA Ops:
  0.0 0.0 copy-start
  0.0 146.0 %ring_kernel.1.returned = f32[256,2048]{1,0:T(8,128)} custom-call(f32[4096,2048]{1,0:T(8,128)} %grad.1, f32[4096,256]{1,0:T(8,128)} %basis.1, f32[2048,512]{1,0:T(8,128)} %in_basis.1, f32[256,512]{1,0:T(8,128)} %eigen.1), custom_call_target="tpu_custom_call" | custom-call | flops 16106127360 | bytes 37748736 | tf_op jit(solution)/shard_map/ring_kernel/pallas_call | solution.py:272
  146.0 0.0 copy-done
  146.0 0.0 copy-start.1
  146.0 1.6 copy-done.1
  147.6 17.4 %expand_kernel.1 = f32[4096,2048]{1,0:T(8,128)} custom-call(f32[4096,256]{1,0:T(8,128)S(1)} %copy-done, f32[256,2048]{1,0:T(8,128)S(1)} %copy-done.1), custom_call_target="tpu_custom_call" | custom-call | flops 12884901888 | bytes 37748736 | tf_op jit(solution)/shard_map/expand_kernel/pallas_call | solution.py:326
Async XLA Ops:
  0.0 146.0 %copy-start = (f32[4096,256]{1,0:T(8,128)S(1)}, f32[4096,256]{1,0:T(8,128)}, u32[]{:S(2)}) copy-start(f32[4096,256]{1,0:T(8,128)} %basis.1) | copy-start | bytes 12582916
  146.0 1.6 copy-start.1

commit v2 on v1

--- a/solution.py
+++ b/solution.py
@@ -11,6 +11,7 @@
 MESH = pl.DeviceIdType.MESH
 RING = 8
 LANES = 128
+STREAMS = 2
 MIB = 1024 * 1024
 
 
@@ -69,13 +70,23 @@
     right = row_of((place + 1) % RING)
     left = row_of((place + RING - 1) % RING)
 
-    def chunk(direction, step):
-        turn = (place + 2 * RING - step) if direction == 0 else (place + step)
-        return pl.multiple_of((turn % RING) * (2 * LANES) + direction * LANES, LANES)
+    half = RING // 2
+
+    def chunk(side, offset):
+        turn = place + RING + (offset if side == 0 else -offset)
+        return pl.multiple_of((turn % RING) * (2 * LANES) + side * LANES, LANES)
+
+    def toward_owner(step):
+        kind, hops = step % 2, step // 2
+        return (1 - kind) * (half - hops) + kind * (hops + 1 - half)
+
+    def from_owner(step):
+        kind, hops = (step + 1) % 2, (step + 1) // 2
+        return (2 * kind - 1) * hops
 
     def fetch(step, direction):
         return pltpu.make_async_copy(
-            grad.at[:, pl.ds(chunk(direction, step), LANES)],
+            grad.at[:, pl.ds(chunk(direction, toward_owner(step)), LANES)],
             grad_buf.at[step % slots, direction],
             grad_sem.at[step % slots, direction],
         )
@@ -127,29 +138,58 @@
     for offset in range(1, RING):
         total_copy(offset).start()
 
-    def hop(ring, send, recv, direction, step):
+    def hop(ring, send, recv, kind, side, step, stream):
+        back = kind if side == 0 else 1 - kind
         return pltpu.make_async_remote_copy(
-            src_ref=ring.at[direction, step],
-            dst_ref=ring.at[direction, step + 1],
-            send_sem=send.at[direction, step],
-            recv_sem=recv.at[direction, step],
-            device_id={"rows": right if direction == 0 else left},
+            src_ref=ring.at[kind, side, step, stream],
+            dst_ref=ring.at[kind, side, step + 1, stream],
+            send_sem=send.at[kind, side, step, stream],
+            recv_sem=recv.at[kind, side, step, stream],
+            device_id={"rows": right + back * (left - right)},
             device_id_type=MESH,
         )
 
+    pieces = [(stream, side) for stream in range(STREAMS) for side in range(2)]
+    band = ring_a.shape[4]
+
     def reduce_step(ring, send, recv, step, local):
-        @pl.when(step == 0)
+        kind, hops = step % 2, step // 2
+
+        def term(stream, side):
+            return local[side][stream * band : (stream + 1) * band, :]
+
+        @pl.when(step < 2)
         def _():
-            for direction in range(2):
-                ring[direction, 0] = local[direction]
-                hop(ring, send, recv, direction, 0).start()
-
-        @pl.when(step > 0)
+            for stream, side in pieces:
+                ring[kind, side, 0, stream] = term(stream, side)
+                hop(ring, send, recv, kind, side, 0, stream).start()
+
+        @pl.when((step >= 2) & (step < RING - 1))
         def _():
-            for direction in range(2):
-                hop(ring, send, recv, direction, step - 1).wait_recv()
-                ring[direction, step] = ring[direction, step] + local[direction]
-                hop(ring, send, recv, direction, step).start()
+            for stream, side in pieces:
+                hop(ring, send, recv, kind, side, hops - 1, stream).wait_recv()
+                ring[kind, side, hops, stream] = ring[kind, side, hops, stream] + term(
+                    stream, side
+                )
+                hop(ring, send, recv, kind, side, hops, stream).start()
+
+        @pl.when(step == RING - 1)
+        def _():
+            for stream, side in pieces:
+                hop(ring, send, recv, 0, side, half - 1, stream).wait_recv()
+                hop(ring, send, recv, 1, side, half - 2, stream).wait_recv()
+                own = (
+                    ring[0, side, half, stream]
+                    + ring[1, side, half - 1, stream]
+                    + term(stream, side)
+                )
+                for way in range(2):
+                    ring[way, side, half, stream] = own
+                    hop(ring, send, recv, way, side, half, stream).start()
+
+    def whole(ring, side, step):
+        kind, hops = (step + 1) % 2, (step + 1) // 2
+        return ring[kind, side, half + hops].reshape(STREAMS * band, LANES)
 
     def project(step, carry):
         fetch(step, 0).wait()
@@ -187,32 +227,34 @@
     load_in.wait()
     rotated[...] = jnp.zeros_like(rotated)
 
-    def basis_rows(step):
+    def basis_rows(offset):
         return jnp.concatenate(
-            [basis_in[pl.ds(chunk(direction, step), LANES), :] for direction in range(2)], axis=0
+            [basis_in[pl.ds(chunk(side, offset), LANES), :] for side in range(2)], axis=0
         )
 
     def arrive(ring, send, recv, step):
-        @pl.when(step >= RING)
+        kind, hops = (step + 1) % 2, (step + 1) // 2
+
+        @pl.when(step > 0)
         def _():
-            for direction in range(2):
-                hop(ring, send, recv, direction, step - 1).wait_recv()
-
-                @pl.when(step < 2 * RING - 2)
+            for stream, side in pieces:
+                hop(ring, send, recv, kind, side, half + hops - 1, stream).wait_recv()
+
+                @pl.when(hops < half - kind)
                 def _():
-                    hop(ring, send, recv, direction, step).start()
+                    hop(ring, send, recv, kind, side, half + hops, stream).start()
 
     def rotate(step, carry):
-        b_high, b_low = split(basis_rows(step))
+        b_high, b_low = split(basis_rows(from_owner(step)))
         arrive(ring_a, send_a, recv_a, step)
-        p_high, p_low = split(jnp.concatenate([ring_a[0, step], ring_a[1, step]], axis=1))
+        p_high, p_low = split(jnp.concatenate([whole(ring_a, 0, step), whole(ring_a, 1, step)], axis=1))
         rotated[...] += dot(
             jnp.concatenate([p_high, p_high, p_low], axis=1),
             jnp.concatenate([b_high, b_low, b_high], axis=0),
         )
         return carry
 
-    lax.fori_loop(RING - 1, 2 * RING - 1, rotate, 0)
+    lax.fori_loop(0, RING, rotate, 0)
 
     swap = pltpu.make_async_remote_copy(
         src_ref=rotated,
@@ -234,7 +276,7 @@
     scaled_low[...] = low
 
     def give_back(step, carry):
-        b_high, b_low = split(basis_rows(step))
+        b_high, b_low = split(basis_rows(toward_owner(step)))
         s_high, s_low = scaled_high[...], scaled_low[...]
         both = ((1,), (1,))
         part = dot(s_high, b_high, both) + dot(s_high, b_low, both) + dot(s_low, b_high, both)
@@ -246,18 +288,23 @@
     def collect(step, carry):
         arrive(ring_b, send_b, recv_b, step)
         for direction in range(2):
-            result[:, pl.ds(chunk(direction, step), LANES)] = ring_b[direction, step]
+            result[:, pl.ds(chunk(direction, from_owner(step)), LANES)] = whole(ring_b, direction, step)
         return carry
 
-    lax.fori_loop(RING - 1, 2 * RING - 1, collect, 0)
+    lax.fori_loop(0, RING, collect, 0)
 
     def drain(step, carry):
-        for direction in range(2):
-            hop(ring_a, send_a, recv_a, direction, step).wait_send()
-            hop(ring_b, send_b, recv_b, direction, step).wait_send()
+        for stream, side in pieces:
+            for ring, send, recv in ((ring_a, send_a, recv_a), (ring_b, send_b, recv_b)):
+                hop(ring, send, recv, 0, side, step, stream).wait_send()
+
+                @pl.when((step != half - 1) & (step != RING - 1))
+                def _():
+                    hop(ring, send, recv, 1, side, step, stream).wait_send()
+
         return carry
 
-    lax.fori_loop(0, 2 * RING - 2, drain, 0)
+    lax.fori_loop(0, RING, drain, 0)
 
 
 def back_rotated(query_grad, out_basis, in_basis, eigenvalues, count):
@@ -265,7 +312,6 @@
     window = out_basis.shape[1]
     directions = in_basis.shape[1]
     slots = 4
-    hops = 2 * RING - 2
     dma = pltpu.SemaphoreType.DMA
     f32, bf16 = jnp.float32, jnp.bfloat16
     flops = 6 * window * columns * (depth + 2 * directions)
@@ -280,8 +326,8 @@
             pltpu.VMEM((window, depth), bf16),
             pltpu.VMEM((columns, directions), f32),
             pltpu.VMEM((window, directions), f32),
-            pltpu.VMEM((2, hops + 1, window, LANES), f32),
-            pltpu.VMEM((2, hops + 1, window, LANES), f32),
+            pltpu.VMEM((2, 2, RING + 1, STREAMS, window // STREAMS, LANES), f32),
+            pltpu.VMEM((2, 2, RING + 1, STREAMS, window // STREAMS, LANES), f32),
             pltpu.VMEM((window, directions), f32),
             pltpu.VMEM((window, directions), f32),
             pltpu.VMEM((window, directions), bf16),
@@ -290,10 +336,10 @@
             pltpu.VMEM((depth, window), f32),
             dma((slots, 2)),
             dma((3,)),
-            dma((2, hops)),
-            dma((2, hops)),
-            dma((2, hops)),
-            dma((2, hops)),
+            dma((2, 2, RING, STREAMS)),
+            dma((2, 2, RING, STREAMS)),
+            dma((2, 2, RING, STREAMS)),
+            dma((2, 2, RING, STREAMS)),
             dma((RING - 1,)),
             dma((RING - 1,)),
             dma,
@@ -322,7 +368,7 @@
 def expand(out_basis, returned):
     depth, window = out_basis.shape
     columns = returned.shape[1]
-    tile = min(512, depth)
+    tile = min(256, depth)
     return pl.pallas_call(
         expand_kernel,
         grid=(depth // tile,),

time: 165 us -> 123 us (0.75)
  Pallas kernels: 163 us -> 122 us
    pallas_call x1, Pallas kernels: 146 us -> 102 us  [back_rotated(): pl.pallas_call(functools.partial(ring_kernel, count), out_shape=jax.Shape...]
    pallas_call x1, Pallas kernels: 17.4 us -> 19.7 us  [expand(): pl.pallas_call(expand_kernel, grid=(depth // tile,), out_shape=jax.ShapeD...]
where the time goes in v2:
time: 123 us
  Pallas kernels  122 us (99%)
  local copies, waits for them, and re-layouts  1.59 us (1%)
    pallas_call x1, Pallas kernels, back_rotated(): pl.pallas_call(functools.partial(ring_kernel, count), out_shape=jax.Shape...  102 us
    pallas_call x1, Pallas kernels, expand(): pl.pallas_call(expand_kernel, grid=(depth // tile,), out_shape=jax.ShapeD...  19.7 us

profile of v2, /device:TPU:0, one launch (start us, length us, event | category | flops | bytes accessed | tf_op | source)
XLA Modules:
  0.0 123.3 jit_solution(10275157713924875728)
XLA Ops:
  0.0 0.0 copy-start
  0.0 102.0 %ring_kernel.1.returned = f32[256,2048]{1,0:T(8,128)} custom-call(f32[4096,2048]{1,0:T(8,128)} %grad.1, f32[4096,256]{1,0:T(8,128)} %basis.1, f32[2048,512]{1,0:T(8,128)} %in_basis.1, f32[256,512]{1,0:T(8,128)} %eigen.1), custom_call_target="tpu_custom_call" | custom-call | flops 16106127360 | bytes 37748736 | tf_op jit(solution)/shard_map/ring_kernel/pallas_call | solution.py:318
  102.0 0.0 copy-done
  102.0 0.0 copy-start.1
  102.0 1.6 %copy-done.1 = f32[256,2048]{1,0:T(8,128)S(1)} copy-done((f32[256,2048]{1,0:T(8,128)S(1)}, f32[256,2048]{1,0:T(8,128)}, u32[]{:S(2)}) %copy-start.1) | copy-done | bytes 2097176
  103.6 19.7 %expand_kernel.1 = f32[4096,2048]{1,0:T(8,128)} custom-call(f32[4096,256]{1,0:T(8,128)S(1)} %copy-done, f32[256,2048]{1,0:T(8,128)S(1)} %copy-done.1), custom_call_target="tpu_custom_call" | custom-call | flops 12884901888 | bytes 37748736 | tf_op jit(solution)/shard_map/expand_kernel/pallas_call | solution.py:372
Async XLA Ops:
  0.0 102.0 %copy-start = (f32[4096,256]{1,0:T(8,128)S(1)}, f32[4096,256]{1,0:T(8,128)}, u32[]{:S(2)}) copy-start(f32[4096,256]{1,0:T(8,128)} %basis.1) | copy-start | bytes 12582916
  102.0 1.6 %copy-start.1 = (f32[256,2048]{1,0:T(8,128)S(1)}, f32[256,2048]{1,0:T(8,128)}, u32[]{:S(2)}) copy-start(f32[256,2048]{1,0:T(8,128)} %ring_kernel.1.returned) | copy-start | bytes 6291460
